TPU v7x, 512 devices: a whole 4x8x8 slice. The times are simulated.
512 devices in a mesh: gx: 32 (over z, x_lo, core), gy: 16 (over x_hi, y).
Axes of the slice: x: 4 (x_hi: 2, x_lo: 2; x = x_hi * 2 + x_lo), y: 8, z: 8, core: 2. Of those that a mesh axis runs over, the one named last changes fastest.
Arguments:
- fields: float32 [2, 2, 16, 1024, 2048], P(None, None, None, 'gx', 'gy'), may hold values from -6 to 6
- wavenumber: float32 [16], P('gy'), may hold values from 0.5 to 2.5
- coupling: float32 [2, 16], P(None, 'gy'), may hold values from -3 to 3
- evanescent: int32 [16, 2048, 1024], P('gy', 'gx'), may hold values 0 or 1
Outputs:
- waves: float32 [2, 2, 16, 1024, 2048], P(None, None, None, 'gx', 'gy')
All inputs are finite; a program needn't handle non-finite values. No bound on the sum of `evanescent` on one device may be relied on, other than what follows from the above.
Results may differ from a plain program's by a relative error of at most 0.000071.
Values sent between devices are 32-bit elements; how exact they have to be, the bound alone decides.
A program may use at most 64 MiB of HBM per device.

v0:
```python
import functools
import math

import jax
import jax.numpy as jnp
import ml_dtypes
import numpy as np
from jax import lax
from jax.experimental import pallas as pl
from jax.experimental.pallas import tpu as pltpu
from jax.sharding import PartitionSpec as P

MESH = pl.DeviceIdType.MESH
NX, NY = 1024, 2048
GX, GY = 32, 16
CH = 4
NT = (((1,), (1,)), ((), ()))
NN = (((1,), (0,)), ((), ()))


def halves(table):
    high = table.astype(ml_dtypes.bfloat16)
    low = (table - high.astype(np.float64)).astype(ml_dtypes.bfloat16)
    return [high, low]


def real_form(angle):
    cos, sin = np.cos(angle), np.sin(angle)
    return np.array([[cos, sin], [-sin, cos]])


def tables():
    form = real_form(2 * np.pi * (np.arange(128)[:, None] * np.arange(128)[None, :] % 128) / 128)
    wave_y = form.reshape(2, 2, 32, 4, 128).transpose(2, 0, 3, 1, 4).reshape(256, 256)
    form = real_form(2 * np.pi * (np.arange(32)[:, None] * np.arange(32)[None, :] % 32) / 32)
    wave_i = np.einsum("qpim,kl->ipkqlm", form, np.eye(4)).reshape(256, 256)
    wave_r = np.einsum("qpmcr,kl->qmkpclr", form.reshape(2, 2, 32, 4, 8), np.eye(8)).reshape(512, 512)
    small = np.stack(halves(wave_y) + halves(wave_i))
    back = wave_r.T.reshape(2, 4, 64, 512).transpose(1, 0, 2, 3).reshape(512, 512)
    large = np.stack(halves(wave_r) + halves(back))
    turn_y = 2 * np.pi * np.arange(16)[:, None] * np.arange(128)[None, :] / NY
    turn_x = 2 * np.pi * np.arange(32)[:, None] * np.tile(np.arange(32), 4)[None, :] / NX
    turns = np.concatenate([np.cos(turn_y), np.sin(turn_y), np.cos(turn_x), np.sin(turn_x)])
    return small, large, turns.astype(np.float32)


def split(value):
    high = value.astype(jnp.bfloat16)
    low = (value - high.astype(jnp.float32)).astype(jnp.bfloat16)
    return high, low


def product(left, right, dims):
    def dot(a, b):
        return lax.dot_general(a, b, dims, preferred_element_type=jnp.float32)

    return dot(left[0], right[0]) + (dot(left[0], right[1]) + dot(left[1], right[0]))


def times(value, cos, sin, orient):
    real, imag = value
    if orient < 0:
        return real * cos + imag * sin, imag * cos - real * sin
    return real * cos - imag * sin, imag * cos + real * sin


def add(a, b):
    return a[0] + b[0], a[1] + b[1]


def sub(a, b):
    return a[0] - b[0], a[1] - b[1]


def quarter(a, orient):
    return (a[1], -a[0]) if orient < 0 else (-a[1], a[0])


def constant_turn(value, step, orient):
    step %= 16
    if step == 0:
        return value
    if step == 4:
        return quarter(value, orient)
    angle = 2 * math.pi * step / 16
    return times(value, math.cos(angle), math.sin(angle), orient)


def four(v, orient):
    a, b = add(v[0], v[2]), sub(v[0], v[2])
    c, d = add(v[1], v[3]), quarter(sub(v[1], v[3]), orient)
    return [add(a, c), add(b, d), sub(a, c), sub(b, d)]


def sixteen(v, orient):
    inner = [four([v[n + 4 * m] for m in range(4)], orient) for n in range(4)]
    out = [None] * 16
    for k in range(4):
        for m, value in enumerate(four([constant_turn(inner[n][k], n * k, orient) for n in range(4)], orient)):
            out[k + 4 * m] = value
    return out


def forward_y(values, turn_cos, turn_sin, table):
    spec = sixteen(values, -1)
    spec = [times(spec[k], turn_cos(k), turn_sin(k), -1) for k in range(16)]
    real = jnp.concatenate([s[0] for s in spec], axis=0)
    imag = jnp.concatenate([s[1] for s in spec], axis=0)
    return product(table, split(jnp.concatenate([real, imag], axis=1)), NT)


def inverse_y(block, turn_cos, turn_sin, table):
    spec = product(split(block.T), table, NN)
    spec = [(spec[8 * k : 8 * k + 8, :128], spec[8 * k : 8 * k + 8, 128:]) for k in range(16)]
    return sixteen([times(spec[k], turn_cos(k), turn_sin(k), 1) for k in range(16)], 1)


def forward_x(block, cos, sin, table):
    spec = product(split(block.T), table, NN)
    value = (spec[:, :128].reshape(16, 8, 128), spec[:, 128:].reshape(16, 8, 128))
    parts = times(value, cos[None], sin[None], -1)
    parts = [part.reshape(128, 128) for part in parts]
    return [jnp.concatenate([part[:64], part[64:]], axis=1) for part in parts]


def inverse_x(value, cos, sin, table):
    parts = [jnp.concatenate([p[:, :128], p[:, 128:]], axis=0).reshape(16, 8, 128) for p in (value[:64], value[64:])]
    parts = times(parts, cos[None], sin[None], 1)
    return product(table, split(jnp.concatenate([p.reshape(128, 128) for p in parts], axis=1)), NT)


def kernel(
    fields, radius, coef, muted, small_in, large_in, turns_in, out,
    small, large, turns, mask, vert, ybuf, xsrc, xbuf, ehigh, elow, vsrc, vbuf, wsrc, local, send, recv,
):
    gx, gy = lax.axis_index("gx"), lax.axis_index("gy")

    loads = [
        pltpu.make_async_copy(muted.at[0], mask, local.at[0]),
        pltpu.make_async_copy(turns_in, turns, local.at[1]),
        pltpu.make_async_copy(small_in, small, local.at[2]),
        pltpu.make_async_copy(large_in, large, local.at[3]),
    ]
    rows = [pl.ds(8 * c, 8) for c in range(CH)]
    own = [pltpu.make_async_copy(fields.at[1, :, gy, rows[c]], ybuf.at[c, gy], local.at[4 + c]) for c in range(CH)]
    for copy in loads + own:
        copy.start()

    barrier = pltpu.get_barrier_semaphore()

    def greet_y(k, carry):
        pl.semaphore_signal(barrier, inc=1, device_id=(gx, lax.rem(gy + k, GY)), device_id_type=MESH)
        return carry

    def greet_x(k, carry):
        pl.semaphore_signal(barrier, inc=1, device_id=(lax.rem(gx + k, GX), gy), device_id_type=MESH)
        return carry

    lax.fori_loop(1, GY, greet_y, 0)
    lax.fori_loop(1, GX, greet_x, 0)
    pl.semaphore_wait(barrier, GX + GY - 2)

    def over_y(phase, c, source, target):
        def one(k, carry):
            peer = lax.rem(gy + k, GY)
            pltpu.make_async_remote_copy(
                src_ref=source(peer), dst_ref=target, send_sem=send.at[phase, c], recv_sem=recv.at[phase, c],
                device_id=(gx, peer), device_id_type=MESH,
            ).start()
            return carry

        lax.fori_loop(1, GY, one, 0)

    def over_x(phase, c, source, target):
        def one(k, carry):
            peer = lax.rem(gx + k, GX)
            pltpu.make_async_remote_copy(
                src_ref=source(peer), dst_ref=target, send_sem=send.at[phase, c], recv_sem=recv.at[phase, c],
                device_id=(peer, gy), device_id_type=MESH,
            ).start()
            return carry

        lax.fori_loop(1, GX, one, 0)

    def wait(buffer, semaphore):
        pltpu.make_async_copy(buffer, buffer, semaphore).wait()

    for c in range(CH):
        over_y(0, c, lambda peer, c=c: fields.at[1, :, peer, rows[c]], ybuf.at[c, gy])

    loads[0].wait()
    lane = lax.broadcasted_iota(jnp.int32, (16, 128), 1)
    row = lax.broadcasted_iota(jnp.int32, (16, 128), 0)
    ky = 64 * gx + 16 * (lane // 32) + row
    ky_wave = (2.0 * math.pi / NY) * jnp.where(ky < NY // 2, ky, ky - NY).astype(jnp.float32)
    square = radius[0] * radius[0]

    def factor(g, carry):
        columns = pl.ds(pl.multiple_of(128 * g, 128), 128)
        for m in range(4):
            picked = None
            for k in range(4):
                piece = mask[16 * k : 16 * k + 16, columns]
                if k != m:
                    piece = pltpu.roll(piece, 32 * (k - m) % 128, 1)
                picked = piece if picked is None else jnp.where(lane // 32 == k, piece, picked)
            kx = lane % 32 + 32 * (4 * g + m)
            kx_wave = (2.0 * math.pi / NX) * jnp.where(kx < NX // 2, kx, kx - NX).astype(jnp.float32)
            depth = jnp.sqrt(jnp.maximum(square - kx_wave * kx_wave - ky_wave * ky_wave, 0.0))
            depth = depth * (1 - picked).astype(jnp.float32)
            place = pl.ds(pl.multiple_of(32 * g + 8 * m, 8), 8)
            vert[place, 0:128] = depth[0:8]
            vert[place, 128:256] = depth[8:16]
        return carry

    lax.fori_loop(0, 8, factor, 0)
    for load in loads[1:]:
        load.wait()

    table_y = (small[0], small[1])
    table_i = (small[2], small[3])

    def turn_y(part):
        return lambda k: turns[16 * part + k : 16 * part + k + 1, :]

    def turn_x(c):
        return turns[pl.ds(32 + 8 * c, 8), :], turns[pl.ds(64 + 8 * c, 8), :]

    for c in range(CH):
        own[c].wait()
        wait(ybuf.at[c, pl.ds(0, GY - 1)], recv.at[0, c])
        values = [(ybuf[c, j, 0], ybuf[c, j, 1]) for j in range(GY)]
        xsrc[c] = forward_y(values, turn_y(0), turn_y(1), table_y).reshape(GX, 8, 128)
        over_x(1, c, lambda peer, c=c: xsrc.at[c, peer], xbuf.at[c, gx])
        xbuf[c, gx] = xsrc[c, gx]

    for c in range(CH):
        wait(xbuf.at[c, pl.ds(0, GX - 1)], recv.at[1, c])
        parts = forward_x(xbuf[c].reshape(256, 128), *turn_x(c), table_i)
        for part in range(2):
            high, low = split(parts[part])
            ehigh[256 * part + 64 * c : 256 * part + 64 * c + 64, :] = high
            elow[256 * part + 64 * c : 256 * part + 64 * c + 64, :] = low

    spec = product((large[0], large[1]), (ehigh[...], elow[...]), NN)
    scale = 0.5 / (NX * NY)
    coef_real, coef_imag = coef[0, 0] * scale, coef[1, 0] * scale
    real, imag = spec[:256], spec[256:]
    depth = vert[...]
    real, imag = (
        depth * coef_real * real - depth * coef_imag * imag,
        depth * coef_real * imag + depth * coef_imag * real,
    )
    high, low = split(jnp.concatenate([real, imag], axis=0))

    for c in range(CH):
        back = (large[2, 128 * c : 128 * c + 128, :], large[3, 128 * c : 128 * c + 128, :])
        value = product(back, (high, low), NN)
        vsrc[c] = inverse_x(value, *turn_x(c), table_i).reshape(GX, 8, 128)
        over_x(2, c, lambda peer, c=c: vsrc.at[c, peer], vbuf.at[c, gx])
        vbuf[c, gx] = vsrc[c, gx]

    for c in range(CH):
        wait(vbuf.at[c, pl.ds(0, GX - 1)], recv.at[2, c])
        values = inverse_y(vbuf[c].reshape(256, 128), turn_y(0), turn_y(1), table_y)
        for j in range(GY):
            wsrc[c, j, 0] = values[j][0]
            wsrc[c, j, 1] = values[j][1]
        over_y(3, c, lambda peer, c=c: wsrc.at[c, peer], out.at[:, gy, rows[c]])
        pltpu.make_async_copy(wsrc.at[c, gy], out.at[:, gy, rows[c]], local.at[8 + c]).start()

    for c in range(CH):
        pltpu.make_async_copy(wsrc.at[c, gy], out.at[:, gy, rows[c]], local.at[8 + c]).wait()
        wait(ybuf.at[c, pl.ds(0, GY - 1)], recv.at[3, c])
        wait(ybuf.at[c, pl.ds(0, GY - 1)], send.at[0, c])
        wait(xbuf.at[c, pl.ds(0, GX - 1)], send.at[1, c])
        wait(vbuf.at[c, pl.ds(0, GX - 1)], send.at[2, c])
        wait(ybuf.at[c, pl.ds(0, GY - 1)], send.at[3, c])


def shards(fields, wavenumber, coupling, evanescent):
    small, large, turns = tables()
    anywhere = pl.BlockSpec(memory_space=pl.ANY)
    scalars = pl.BlockSpec(memory_space=pltpu.SMEM)
    wave = pl.pallas_call(
        kernel,
        out_shape=jax.ShapeDtypeStruct((2, GY, 32, 128), jnp.float32),
        in_specs=[anywhere, scalars, scalars, anywhere, anywhere, anywhere, anywhere],
        out_specs=anywhere,
        scratch_shapes=[
            pltpu.VMEM((4, 256, 256), jnp.bfloat16),
            pltpu.VMEM((4, 512, 512), jnp.bfloat16),
            pltpu.VMEM((96, 128), jnp.float32),
            pltpu.VMEM((64, 1024), jnp.int32),
            pltpu.VMEM((256, 256), jnp.float32),
            pltpu.VMEM((CH, GY, 2, 8, 128), jnp.float32),
            pltpu.VMEM((CH, GX, 8, 128), jnp.float32),
            pltpu.VMEM((CH, GX, 8, 128), jnp.float32),
            pltpu.VMEM((512, 256), jnp.bfloat16),
            pltpu.VMEM((512, 256), jnp.bfloat16),
            pltpu.VMEM((CH, GX, 8, 128), jnp.float32),
            pltpu.VMEM((CH, GX, 8, 128), jnp.float32),
            pltpu.VMEM((CH, GY, 2, 8, 128), jnp.float32),
            pltpu.SemaphoreType.DMA((12,)),
            pltpu.SemaphoreType.DMA((4, CH)),
            pltpu.SemaphoreType.DMA((4, CH)),
        ],
        compiler_params=pltpu.CompilerParams(
            collective_id=0, has_side_effects=True, vmem_limit_bytes=48 * 1024 * 1024
        ),
    )(fields, wavenumber, coupling, evanescent, jnp.asarray(small), jnp.asarray(large), jnp.asarray(turns))
    press = 0.5 * fields[0]
    return jnp.stack([press - wave, press + wave])


def solution(mesh):
    in_specs = (P(None, None, None, "gx", "gy"), P("gy"), P(None, "gy"), P("gy", "gx", None))
    out_specs = P(None, None, None, "gx", "gy")
    return jax.shard_map(shards, mesh=mesh, in_specs=in_specs, out_specs=out_specs, check_vma=False)
```

profile of v0, /device:TPU:1, one launch (start us, length us, event | category | flops | bytes accessed | tf_op | source)
XLA Modules:
  0.0 71.3 jit_solution(14351551857612858909)
XLA Ops:
  0.7 0.7 %copy.8.coef = f32[2,1]{1,0:T(2,128)S(1)} copy(f32[2,1]{0,1:T(1,128)} %param.9) | data formatting | bytes 16 | tf_op args[2]
  1.4 0.0 copy-start
  1.4 1.2 %copy-done = f32[2,2,16,32,128]{4,3,2,1,0:T(8,128)S(1)} copy-done((f32[2,2,16,32,128]{4,3,2,1,0:T(8,128)S(1)}, f32[2,2,16,32,128]{4,3,2,1,0:T(8,128)}, u32[]{:S(2)}) %copy-start) | copy-done | bytes 1048600
  2.6 0.0 copy-start.1
  2.6 1.6 %copy-done.1 = bf16[4,512,512]{2,1,0:T(8,128)(2,1)S(1)} copy-done((bf16[4,512,512]{2,1,0:T(8,128)(2,1)S(1)}, bf16[4,512,512]{2,1,0:T(8,128)(2,1)}, u32[]{:S(2)}) %copy-start.1) | copy-done | bytes 2097176
  4.2 0.0 copy-start.2
  4.2 1.0 %copy-done.2 = bf16[4,256,256]{2,1,0:T(8,128)(2,1)S(1)} copy-done((bf16[4,256,256]{2,1,0:T(8,128)(2,1)S(1)}, bf16[4,256,256]{2,1,0:T(8,128)(2,1)}, u32[]{:S(2)}) %copy-start.2) | copy-done | bytes 524312
  5.3 0.0 copy-start.3
  5.3 0.9 %copy-done.3 = s32[1,64,1024]{2,1,0:T(8,128)S(1)} copy-done((s32[1,64,1024]{2,1,0:T(8,128)S(1)}, s32[1,64,1024]{2,1,0:T(8,128)}, u32[]{:S(2)}) %copy-start.3) | copy-done | bytes 262168
  6.2 0.0 copy-start.4
  6.2 0.8 %copy-done.4 = f32[96,128]{1,0:T(8,128)S(1)} copy-done((f32[96,128]{1,0:T(8,128)S(1)}, f32[96,128]{1,0:T(8,128)}, u32[]{:S(2)}) %copy-start.4) | copy-done | bytes 49176
  7.0 63.1 %shard_map.73 = f32[2,16,32,128]{3,2,1,0:T(8,128)S(1)} custom-call(f32[2,2,16,32,128]{4,3,2,1,0:T(8,128)S(1)} %copy-done, f32[1]{0:T(128)S(6)} %copy.9.radius, f32[2,1]{1,0:T(2,128)S(1)} %copy.8.coef, s32[1,64,1024]{2,1,0:T(8,128)S(1)} %copy-done.3, bf16[4,256,256]{2,1,0:T(8,128)(2,1)S(1)} %copy-done.2, bf16[4,512,512]{2,1,0:T(8,128)(2,1)S(1)} %copy-done.1, ...), custom_call_target="tpu_custom_call" | custom-call | tf_op jit(solution)/shard_map/pallas_call | solution.py:285
  70.1 0.1 fusion
  70.3 1.0 %pad_maximum_fusion = f32[2,2,16,32,128]{4,3,2,1,0:T(8,128)} fusion(f32[1,2,16,32,128]{4,3,2,1,0:T(8,128)S(1)} %get-tuple-element.6, f32[1,2,16,32,128]{4,3,2,1,0:T(8,128)S(1)} %get-tuple-element.5), kind=kLoop, calls=%fused_computation | loop fusion | flops 262144 | bytes 2097152 | tf_op jit(solution)/shard_map/stack | solution.py:313
Async XLA Ops:
  1.4 1.2 %copy-start = (f32[2,2,16,32,128]{4,3,2,1,0:T(8,128)S(1)}, f32[2,2,16,32,128]{4,3,2,1,0:T(8,128)}, u32[]{:S(2)}) copy-start(f32[2,2,16,32,128]{4,3,2,1,0:T(8,128)} %fields.1) | copy-start | bytes 3145732
  2.6 1.6 %copy-start.1 = (bf16[4,512,512]{2,1,0:T(8,128)(2,1)S(1)}, bf16[4,512,512]{2,1,0:T(8,128)(2,1)}, u32[]{:S(2)}) copy-start(bf16[4,512,512]{2,1,0:T(8,128)(2,1)} %constant.9.clone.large_in) | copy-start | bytes 6291460
  4.2 1.0 %copy-start.2 = (bf16[4,256,256]{2,1,0:T(8,128)(2,1)S(1)}, bf16[4,256,256]{2,1,0:T(8,128)(2,1)}, u32[]{:S(2)}) copy-start(bf16[4,256,256]{2,1,0:T(8,128)(2,1)} %constant.8.clone.small_in) | copy-start | bytes 1572868
  5.3 0.9 %copy-start.3 = (s32[1,64,1024]{2,1,0:T(8,128)S(1)}, s32[1,64,1024]{2,1,0:T(8,128)}, u32[]{:S(2)}) copy-start(s32[1,64,1024]{2,1,0:T(8,128)} %muted.1) | copy-start | bytes 786436
  6.2 0.8 %copy-start.4 = (f32[96,128]{1,0:T(8,128)S(1)}, f32[96,128]{1,0:T(8,128)}, u32[]{:S(2)}) copy-start(f32[96,128]{1,0:T(8,128)} %constant.10.clone.turns_in) | copy-start | bytes 147460
where the time goes:
time: 71.6 us; the launch traced here: 71.3 us
  Pallas kernels  63.1 us (88%)
  local copies, waits for them, and re-layouts  6.35 us (9%)
  other arithmetic  1.17 us (2%)
    pallas_call x1, Pallas kernels, shards(): pl.pallas_call(kernel, out_shape=jax.ShapeDtypeStruct((2, GY, 32, 128), j...  63.1 us
    unnamed x11, local copies, waits for them, and re-layouts  6.35 us

commit v1 on v0

--- a/solution.py
+++ b/solution.py
@@ -14,6 +14,10 @@
 NX, NY = 1024, 2048
 GX, GY = 32, 16
 CH = 4
+AHEAD = 4
+TOP = int(2.5 * NY / (2 * math.pi))
+IDLE_FROM, IDLE_TO = TOP // 64 + 1, (NY - TOP) // 64
+BUSY = GX - (IDLE_TO - IDLE_FROM)
 NT = (((1,), (1,)), ((), ()))
 NN = (((1,), (0,)), ((), ()))
 
@@ -131,9 +135,38 @@
 
 def kernel(
     fields, radius, coef, muted, small_in, large_in, turns_in, out,
-    small, large, turns, mask, vert, ybuf, xsrc, xbuf, ehigh, elow, vsrc, vbuf, wsrc, local, send, recv,
+    small, large, turns, mask, vert, vel, ybuf, xsrc, xbuf, ehigh, elow, vsrc, vbuf, wsrc, local, send, recv,
 ):
     gx, gy = lax.axis_index("gx"), lax.axis_index("gy")
+    busy = jnp.logical_or(gx < IDLE_FROM, gx >= IDLE_TO)
+    idle = jnp.logical_not(busy)
+    barrier = pltpu.get_barrier_semaphore()
+
+    load_vel = pltpu.make_async_copy(fields.at[1], vel, local.at[4])
+    load_vel.start()
+
+    def peer_y(k):
+        turn = (k - 1) // 2
+        far = 4 - (turn + 1) // 2
+        y = lax.rem(gy + 8 + jnp.where(lax.rem(turn, 2) == 1, far, -far), 8)
+        return 8 * lax.rem(gy // 8 + k, 2) + y
+
+    def peer_x(k):
+        turn = k // 4
+        far = 4 - (turn + 1) // 2
+        z = lax.rem(gx // 4 + 8 + jnp.where(lax.rem(turn, 2) == 1, far, -far), 8)
+        return 4 * z + lax.rem(gx + 3 - lax.rem(k, 4), 4)
+
+    def greet_y(k, carry):
+        pl.semaphore_signal(barrier, inc=1, device_id=(gx, peer_y(k)), device_id_type=MESH)
+        return carry
+
+    def greet_x(k, carry):
+        pl.semaphore_signal(barrier, inc=1, device_id=(peer_x(k), gy), device_id_type=MESH)
+        return carry
+
+    lax.fori_loop(0, GX - 1, greet_x, 0)
+    lax.fori_loop(1, GY, greet_y, 0)
 
     loads = [
         pltpu.make_async_copy(muted.at[0], mask, local.at[0]),
@@ -142,27 +175,10 @@
         pltpu.make_async_copy(large_in, large, local.at[3]),
     ]
     rows = [pl.ds(8 * c, 8) for c in range(CH)]
-    own = [pltpu.make_async_copy(fields.at[1, :, gy, rows[c]], ybuf.at[c, gy], local.at[4 + c]) for c in range(CH)]
-    for copy in loads + own:
-        copy.start()
-
-    barrier = pltpu.get_barrier_semaphore()
-
-    def greet_y(k, carry):
-        pl.semaphore_signal(barrier, inc=1, device_id=(gx, lax.rem(gy + k, GY)), device_id_type=MESH)
-        return carry
-
-    def greet_x(k, carry):
-        pl.semaphore_signal(barrier, inc=1, device_id=(lax.rem(gx + k, GX), gy), device_id_type=MESH)
-        return carry
-
-    lax.fori_loop(1, GY, greet_y, 0)
-    lax.fori_loop(1, GX, greet_x, 0)
-    pl.semaphore_wait(barrier, GX + GY - 2)
 
     def over_y(phase, c, source, target):
         def one(k, carry):
-            peer = lax.rem(gy + k, GY)
+            peer = peer_y(k)
             pltpu.make_async_remote_copy(
                 src_ref=source(peer), dst_ref=target, send_sem=send.at[phase, c], recv_sem=recv.at[phase, c],
                 device_id=(gx, peer), device_id_type=MESH,
@@ -171,24 +187,37 @@
 
         lax.fori_loop(1, GY, one, 0)
 
-    def over_x(phase, c, source, target):
+    def over_x(phase, c, source, target, busy_only):
         def one(k, carry):
-            peer = lax.rem(gx + k, GX)
-            pltpu.make_async_remote_copy(
-                src_ref=source(peer), dst_ref=target, send_sem=send.at[phase, c], recv_sem=recv.at[phase, c],
-                device_id=(peer, gy), device_id_type=MESH,
-            ).start()
+            peer = peer_x(k)
+
+            def go():
+                pltpu.make_async_remote_copy(
+                    src_ref=source(peer), dst_ref=target, send_sem=send.at[phase, c], recv_sem=recv.at[phase, c],
+                    device_id=(peer, gy), device_id_type=MESH,
+                ).start()
+
+            if busy_only:
+                pl.when(jnp.logical_or(peer < IDLE_FROM, peer >= IDLE_TO))(go)
+            else:
+                go()
             return carry
 
-        lax.fori_loop(1, GX, one, 0)
+        lax.fori_loop(0, GX - 1, one, 0)
 
     def wait(buffer, semaphore):
         pltpu.make_async_copy(buffer, buffer, semaphore).wait()
 
-    for c in range(CH):
-        over_y(0, c, lambda peer, c=c: fields.at[1, :, peer, rows[c]], ybuf.at[c, gy])
-
-    loads[0].wait()
+    def first_y(c):
+        over_y(0, c, lambda peer: vel.at[:, peer, rows[c]], ybuf.at[c, gy])
+
+    load_vel.wait()
+    pl.semaphore_wait(barrier, GX + GY - 2)
+    for c in range(AHEAD):
+        first_y(c)
+    for load in loads:
+        load.start()
+
     lane = lax.broadcasted_iota(jnp.int32, (16, 128), 1)
     row = lax.broadcasted_iota(jnp.int32, (16, 128), 0)
     ky = 64 * gx + 16 * (lane // 32) + row
@@ -213,9 +242,12 @@
             vert[place, 128:256] = depth[8:16]
         return carry
 
+    for c in range(CH):
+        ybuf[c, gy] = vel[:, gy, rows[c]]
+        vbuf[c, IDLE_FROM:IDLE_TO] = jnp.zeros((IDLE_TO - IDLE_FROM, 8, 128), jnp.float32)
+    for load in loads:
+        load.wait()
     lax.fori_loop(0, 8, factor, 0)
-    for load in loads[1:]:
-        load.wait()
 
     table_y = (small[0], small[1])
     table_i = (small[2], small[3])
@@ -227,72 +259,78 @@
         return turns[pl.ds(32 + 8 * c, 8), :], turns[pl.ds(64 + 8 * c, 8), :]
 
     for c in range(CH):
-        own[c].wait()
         wait(ybuf.at[c, pl.ds(0, GY - 1)], recv.at[0, c])
+        if c + AHEAD < CH:
+            first_y(c + AHEAD)
         values = [(ybuf[c, j, 0], ybuf[c, j, 1]) for j in range(GY)]
         xsrc[c] = forward_y(values, turn_y(0), turn_y(1), table_y).reshape(GX, 8, 128)
-        over_x(1, c, lambda peer, c=c: xsrc.at[c, peer], xbuf.at[c, gx])
+        over_x(1, c, lambda peer: xsrc.at[c, peer], xbuf.at[c, gx], True)
         xbuf[c, gx] = xsrc[c, gx]
 
+    @pl.when(busy)
+    def spectrum():
+        for c in range(CH):
+            wait(xbuf.at[c, pl.ds(0, GX - 1)], recv.at[1, c])
+            parts = forward_x(xbuf[c].reshape(256, 128), *turn_x(c), table_i)
+            for part in range(2):
+                high, low = split(parts[part])
+                ehigh[256 * part + 64 * c : 256 * part + 64 * c + 64, :] = high
+                elow[256 * part + 64 * c : 256 * part + 64 * c + 64, :] = low
+
+        spec = product((large[0], large[1]), (ehigh[...], elow[...]), NN)
+        scale = 0.5 / (NX * NY)
+        coef_real, coef_imag = coef[0] * scale, coef[1] * scale
+        real, imag = spec[:256], spec[256:]
+        depth = vert[...]
+        real, imag = (
+            depth * coef_real * real - depth * coef_imag * imag,
+            depth * coef_real * imag + depth * coef_imag * real,
+        )
+        high, low = split(jnp.concatenate([real, imag], axis=0))
+
+        for c in range(CH):
+            back = (large[2, 128 * c : 128 * c + 128, :], large[3, 128 * c : 128 * c + 128, :])
+            value = product(back, (high, low), NN)
+            vsrc[c] = inverse_x(value, *turn_x(c), table_i).reshape(GX, 8, 128)
+            over_x(2, c, lambda peer: vsrc.at[c, peer], vbuf.at[c, gx], False)
+            vbuf[c, gx] = vsrc[c, gx]
+
     for c in range(CH):
-        wait(xbuf.at[c, pl.ds(0, GX - 1)], recv.at[1, c])
-        parts = forward_x(xbuf[c].reshape(256, 128), *turn_x(c), table_i)
-        for part in range(2):
-            high, low = split(parts[part])
-            ehigh[256 * part + 64 * c : 256 * part + 64 * c + 64, :] = high
-            elow[256 * part + 64 * c : 256 * part + 64 * c + 64, :] = low
-
-    spec = product((large[0], large[1]), (ehigh[...], elow[...]), NN)
-    scale = 0.5 / (NX * NY)
-    coef_real, coef_imag = coef[0, 0] * scale, coef[1, 0] * scale
-    real, imag = spec[:256], spec[256:]
-    depth = vert[...]
-    real, imag = (
-        depth * coef_real * real - depth * coef_imag * imag,
-        depth * coef_real * imag + depth * coef_imag * real,
-    )
-    high, low = split(jnp.concatenate([real, imag], axis=0))
-
-    for c in range(CH):
-        back = (large[2, 128 * c : 128 * c + 128, :], large[3, 128 * c : 128 * c + 128, :])
-        value = product(back, (high, low), NN)
-        vsrc[c] = inverse_x(value, *turn_x(c), table_i).reshape(GX, 8, 128)
-        over_x(2, c, lambda peer, c=c: vsrc.at[c, peer], vbuf.at[c, gx])
-        vbuf[c, gx] = vsrc[c, gx]
-
-    for c in range(CH):
-        wait(vbuf.at[c, pl.ds(0, GX - 1)], recv.at[2, c])
+        pl.when(busy)(lambda: wait(vbuf.at[c, pl.ds(0, BUSY - 1)], recv.at[2, c]))
+        pl.when(idle)(lambda: wait(vbuf.at[c, pl.ds(0, BUSY)], recv.at[2, c]))
         values = inverse_y(vbuf[c].reshape(256, 128), turn_y(0), turn_y(1), table_y)
         for j in range(GY):
             wsrc[c, j, 0] = values[j][0]
             wsrc[c, j, 1] = values[j][1]
-        over_y(3, c, lambda peer, c=c: wsrc.at[c, peer], out.at[:, gy, rows[c]])
-        pltpu.make_async_copy(wsrc.at[c, gy], out.at[:, gy, rows[c]], local.at[8 + c]).start()
+        over_y(3, c, lambda peer: wsrc.at[c, peer], out.at[:, gy, rows[c]])
+        pltpu.make_async_copy(wsrc.at[c, gy], out.at[:, gy, rows[c]], local.at[5 + c]).start()
 
     for c in range(CH):
-        pltpu.make_async_copy(wsrc.at[c, gy], out.at[:, gy, rows[c]], local.at[8 + c]).wait()
+        wait(ybuf.at[c, pl.ds(0, GY - 1)], send.at[0, c])
+        pl.when(busy)(lambda: wait(xbuf.at[c, pl.ds(0, BUSY - 1)], send.at[1, c]))
+        pl.when(idle)(lambda: wait(xbuf.at[c, pl.ds(0, BUSY)], send.at[1, c]))
+        pl.when(busy)(lambda: wait(vbuf.at[c, pl.ds(0, GX - 1)], send.at[2, c]))
+        pltpu.make_async_copy(wsrc.at[c, gy], out.at[:, gy, rows[c]], local.at[5 + c]).wait()
+        wait(ybuf.at[c, pl.ds(0, GY - 1)], send.at[3, c])
         wait(ybuf.at[c, pl.ds(0, GY - 1)], recv.at[3, c])
-        wait(ybuf.at[c, pl.ds(0, GY - 1)], send.at[0, c])
-        wait(xbuf.at[c, pl.ds(0, GX - 1)], send.at[1, c])
-        wait(vbuf.at[c, pl.ds(0, GX - 1)], send.at[2, c])
-        wait(ybuf.at[c, pl.ds(0, GY - 1)], send.at[3, c])
 
 
 def shards(fields, wavenumber, coupling, evanescent):
     small, large, turns = tables()
-    anywhere = pl.BlockSpec(memory_space=pl.ANY)
+    hbm = pl.BlockSpec(memory_space=pltpu.HBM)
     scalars = pl.BlockSpec(memory_space=pltpu.SMEM)
     wave = pl.pallas_call(
         kernel,
-        out_shape=jax.ShapeDtypeStruct((2, GY, 32, 128), jnp.float32),
-        in_specs=[anywhere, scalars, scalars, anywhere, anywhere, anywhere, anywhere],
-        out_specs=anywhere,
+        out_shape=pltpu.VMEM((2, GY, 32, 128), jnp.float32),
+        in_specs=[hbm, scalars, scalars, hbm, hbm, hbm, hbm],
+        out_specs=pl.BlockSpec(memory_space=pl.ANY),
         scratch_shapes=[
             pltpu.VMEM((4, 256, 256), jnp.bfloat16),
             pltpu.VMEM((4, 512, 512), jnp.bfloat16),
             pltpu.VMEM((96, 128), jnp.float32),
             pltpu.VMEM((64, 1024), jnp.int32),
             pltpu.VMEM((256, 256), jnp.float32),
+            pltpu.VMEM((2, GY, 32, 128), jnp.float32),
             pltpu.VMEM((CH, GY, 2, 8, 128), jnp.float32),
             pltpu.VMEM((CH, GX, 8, 128), jnp.float32),
             pltpu.VMEM((CH, GX, 8, 128), jnp.float32),
@@ -306,9 +344,9 @@
             pltpu.SemaphoreType.DMA((4, CH)),
         ],
         compiler_params=pltpu.CompilerParams(
-            collective_id=0, has_side_effects=True, vmem_limit_bytes=48 * 1024 * 1024
+            collective_id=0, has_side_effects=True, vmem_limit_bytes=60 * 1024 * 1024
         ),
-    )(fields, wavenumber, coupling, evanescent, jnp.asarray(small), jnp.asarray(large), jnp.asarray(turns))
+    )(fields, wavenumber, coupling.reshape(2), evanescent, jnp.asarray(small), jnp.asarray(large), jnp.asarray(turns))
     press = 0.5 * fields[0]
     return jnp.stack([press - wave, press + wave])
 

time: 71.6 us -> 65.7 us (0.918)
  local copies, waits for them, and re-layouts: 6.35 us -> 0.01 us
    unnamed x11 -> x2, local copies, waits for them, and re-layouts: 6.35 us -> 0.01 us
where the time goes in v1:
time: 65.7 us; the launch traced here: 65.6 us
  Pallas kernels  63.7 us (97%)
  other arithmetic  1.18 us (2%)
  between operations  0.68 us (1%)
    pallas_call x1, Pallas kernels, shards(): pl.pallas_call(kernel, out_shape=pltpu.VMEM((2, GY, 32, 128), jnp.float32...  63.7 us

profile of v1, /device:TPU:1, one launch (start us, length us, event | category | flops | bytes accessed | tf_op | source)
XLA Modules:
  0.0 65.6 jit_solution(9820547258939278143)
XLA Ops:
  0.7 0.0 copy-start
  0.7 63.7 %shard_map.73 = f32[2,16,32,128]{3,2,1,0:T(8,128)S(1)} custom-call(f32[2,2,16,32,128]{4,3,2,1,0:T(8,128)} %fields.1, f32[1]{0:T(128)S(6)} %copy.8.radius, f32[2]{0:T(128)} %bitcast.12, s32[1,64,1024]{2,1,0:T(8,128)} %muted.1, bf16[4,256,256]{2,1,0:T(8,128)(2,1)} %constant.8.clone.small_in, bf16[4,512,512]{2,1,0:T(8,128)(2,1)} %constant.9.clone.large_in, ...), custom_call_target="tpu_custom_call" | custom-call | tf_op jit(solution)/shard_map/pallas_call | solution.py:322
  64.4 0.0 copy-done
  64.4 0.1 fusion
  64.5 1.0 %pad_maximum_fusion = f32[2,2,16,32,128]{4,3,2,1,0:T(8,128)} fusion(f32[1,2,16,32,128]{4,3,2,1,0:T(8,128)S(1)} %get-tuple-element.6, f32[1,2,16,32,128]{4,3,2,1,0:T(8,128)S(1)} %get-tuple-element.5), kind=kLoop, calls=%fused_computation | loop fusion | flops 262144 | bytes 2097152 | tf_op jit(solution)/shard_map/stack | solution.py:351
Async XLA Ops:
  0.7 63.7 %copy-start = (f32[2,2,16,32,128]{4,3,2,1,0:T(8,128)S(1)}, f32[2,2,16,32,128]{4,3,2,1,0:T(8,128)}, u32[]{:S(2)}) copy-start(f32[2,2,16,32,128]{4,3,2,1,0:T(8,128)} %fields.1) | copy-start | bytes 3145732

commit v2 on v1

--- a/solution.py
+++ b/solution.py
@@ -157,6 +157,14 @@
         z = lax.rem(gx // 4 + 8 + jnp.where(lax.rem(turn, 2) == 1, far, -far), 8)
         return 4 * z + lax.rem(gx + 3 - lax.rem(k, 4), 4)
 
+    def early_x(k):
+        return 4 * (k // 4) + lax.rem(gx + k, 4)
+
+    def early_y(k):
+        step = k // 2
+        y = lax.rem(9 + jnp.where(lax.rem(step, 2) == 1, -((step + 1) // 2), step // 2), 8)
+        return 8 * lax.rem(gy // 8 + k, 2) + y
+
     def greet_y(k, carry):
         pl.semaphore_signal(barrier, inc=1, device_id=(gx, peer_y(k)), device_id_type=MESH)
         return carry
@@ -165,8 +173,8 @@
         pl.semaphore_signal(barrier, inc=1, device_id=(peer_x(k), gy), device_id_type=MESH)
         return carry
 
-    lax.fori_loop(0, GX - 1, greet_x, 0)
-    lax.fori_loop(1, GY, greet_y, 0)
+    lax.fori_loop(1, GY, greet_y, 0, unroll=True)
+    lax.fori_loop(0, GX - 1, greet_x, 0, unroll=True)
 
     loads = [
         pltpu.make_async_copy(muted.at[0], mask, local.at[0]),
@@ -178,18 +186,22 @@
 
     def over_y(phase, c, source, target):
         def one(k, carry):
-            peer = peer_y(k)
-            pltpu.make_async_remote_copy(
+            peer = peer_y(k + 1) if phase == 0 else early_y(k)
+
+            def go():
+                pltpu.make_async_remote_copy(
                 src_ref=source(peer), dst_ref=target, send_sem=send.at[phase, c], recv_sem=recv.at[phase, c],
                 device_id=(gx, peer), device_id_type=MESH,
-            ).start()
+                ).start()
+
+            pl.when(peer != gy)(go)
             return carry
 
-        lax.fori_loop(1, GY, one, 0)
+        lax.fori_loop(0, GY, one, 0)
 
     def over_x(phase, c, source, target, busy_only):
         def one(k, carry):
-            peer = peer_x(k)
+            peer = peer_x(k) if busy_only else early_x(k)
 
             def go():
                 pltpu.make_async_remote_copy(
@@ -200,10 +212,10 @@
             if busy_only:
                 pl.when(jnp.logical_or(peer < IDLE_FROM, peer >= IDLE_TO))(go)
             else:
-                go()
+                pl.when(peer != gx)(go)
             return carry
 
-        lax.fori_loop(0, GX - 1, one, 0)
+        lax.fori_loop(0, GX, one, 0) if not busy_only else lax.fori_loop(0, GX - 1, one, 0)
 
     def wait(buffer, semaphore):
         pltpu.make_async_copy(buffer, buffer, semaphore).wait()

time: 65.7 us -> 62.5 us (0.951)
  Pallas kernels: 63.7 us -> 60.4 us
    pallas_call x1, Pallas kernels: 63.7 us -> 60.4 us  [shards(): pl.pallas_call(kernel, out_shape=pltpu.VMEM((2, GY, 32, 128), jnp.float32...]
where the time goes in v2:
time: 62.5 us; the launch traced here: 62.2 us
  Pallas kernels  60.4 us (97%)
  other arithmetic  1.18 us (2%)
  between operations  0.68 us (1%)
    pallas_call x1, Pallas kernels, shards(): pl.pallas_call(kernel, out_shape=pltpu.VMEM((2, GY, 32, 128), jnp.float32...  60.4 us

profile of v2, /device:TPU:1, one launch (start us, length us, event | category | flops | bytes accessed | tf_op | source)
XLA Modules:
  0.0 62.2 jit_solution(369481602521250772)
XLA Ops:
  0.7 0.0 copy-start
  0.7 60.4 %shard_map.73 = f32[2,16,32,128]{3,2,1,0:T(8,128)S(1)} custom-call(f32[2,2,16,32,128]{4,3,2,1,0:T(8,128)} %fields.1, f32[1]{0:T(128)S(6)} %copy.8.radius, f32[2]{0:T(128)} %bitcast.12, s32[1,64,1024]{2,1,0:T(8,128)} %muted.1, bf16[4,256,256]{2,1,0:T(8,128)(2,1)} %constant.8.clone.small_in, bf16[4,512,512]{2,1,0:T(8,128)(2,1)} %constant.9.clone.large_in, ...), custom_call_target="tpu_custom_call" | custom-call | tf_op jit(solution)/shard_map/pallas_call | solution.py:334
  61.1 0.0 copy-done
  61.1 0.1 fusion
  61.2 1.0 %pad_maximum_fusion = f32[2,2,16,32,128]{4,3,2,1,0:T(8,128)} fusion(f32[1,2,16,32,128]{4,3,2,1,0:T(8,128)S(1)} %get-tuple-element.6, f32[1,2,16,32,128]{4,3,2,1,0:T(8,128)S(1)} %get-tuple-element.5), kind=kLoop, calls=%fused_computation | loop fusion | flops 262144 | bytes 2097152 | tf_op jit(solution)/shard_map/stack | solution.py:363
Async XLA Ops:
  0.7 60.4 %copy-start = (f32[2,2,16,32,128]{4,3,2,1,0:T(8,128)S(1)}, f32[2,2,16,32,128]{4,3,2,1,0:T(8,128)}, u32[]{:S(2)}) copy-start(f32[2,2,16,32,128]{4,3,2,1,0:T(8,128)} %fields.1) | copy-start | bytes 3145732

commit v3 on v2

--- a/solution.py
+++ b/solution.py
@@ -14,7 +14,6 @@
 NX, NY = 1024, 2048
 GX, GY = 32, 16
 CH = 4
-AHEAD = 4
 TOP = int(2.5 * NY / (2 * math.pi))
 IDLE_FROM, IDLE_TO = TOP // 64 + 1, (NY - TOP) // 64
 BUSY = GX - (IDLE_TO - IDLE_FROM)
@@ -38,10 +37,9 @@
     wave_y = form.reshape(2, 2, 32, 4, 128).transpose(2, 0, 3, 1, 4).reshape(256, 256)
     form = real_form(2 * np.pi * (np.arange(32)[:, None] * np.arange(32)[None, :] % 32) / 32)
     wave_i = np.einsum("qpim,kl->ipkqlm", form, np.eye(4)).reshape(256, 256)
-    wave_r = np.einsum("qpmcr,kl->qmkpclr", form.reshape(2, 2, 32, 4, 8), np.eye(8)).reshape(512, 512)
+    wave_r = np.einsum("qpmcr,kl->qmkcplr", form.reshape(2, 2, 32, 4, 8), np.eye(8)).reshape(512, 512)
     small = np.stack(halves(wave_y) + halves(wave_i))
-    back = wave_r.T.reshape(2, 4, 64, 512).transpose(1, 0, 2, 3).reshape(512, 512)
-    large = np.stack(halves(wave_r) + halves(back))
+    large = np.stack(halves(wave_r) + halves(wave_r.T))
     turn_y = 2 * np.pi * np.arange(16)[:, None] * np.arange(128)[None, :] / NY
     turn_x = 2 * np.pi * np.arange(32)[:, None] * np.tile(np.arange(32), 4)[None, :] / NX
     turns = np.concatenate([np.cos(turn_y), np.sin(turn_y), np.cos(turn_x), np.sin(turn_x)])
@@ -184,22 +182,22 @@
     ]
     rows = [pl.ds(8 * c, 8) for c in range(CH)]
 
-    def over_y(phase, c, source, target):
+    def over_y(phase, c, source, target, start=0, stop=GY):
         def one(k, carry):
             peer = peer_y(k + 1) if phase == 0 else early_y(k)
 
             def go():
                 pltpu.make_async_remote_copy(
-                src_ref=source(peer), dst_ref=target, send_sem=send.at[phase, c], recv_sem=recv.at[phase, c],
-                device_id=(gx, peer), device_id_type=MESH,
+                    src_ref=source(peer), dst_ref=target, send_sem=send.at[phase, c], recv_sem=recv.at[phase, c],
+                    device_id=(gx, peer), device_id_type=MESH,
                 ).start()
 
             pl.when(peer != gy)(go)
             return carry
 
-        lax.fori_loop(0, GY, one, 0)
-
-    def over_x(phase, c, source, target, busy_only):
+        lax.fori_loop(start, stop, one, 0, unroll=True)
+
+    def over_x(phase, c, source, target, busy_only, start=0, stop=GX):
         def one(k, carry):
             peer = peer_x(k) if busy_only else early_x(k)
 
@@ -215,7 +213,7 @@
                 pl.when(peer != gx)(go)
             return carry
 
-        lax.fori_loop(0, GX, one, 0) if not busy_only else lax.fori_loop(0, GX - 1, one, 0)
+        lax.fori_loop(start, stop, one, 0, unroll=True)
 
     def wait(buffer, semaphore):
         pltpu.make_async_copy(buffer, buffer, semaphore).wait()
@@ -225,7 +223,7 @@
 
     load_vel.wait()
     pl.semaphore_wait(barrier, GX + GY - 2)
-    for c in range(AHEAD):
+    for c in range(CH):
         first_y(c)
     for load in loads:
         load.start()
@@ -272,11 +270,9 @@
 
     for c in range(CH):
         wait(ybuf.at[c, pl.ds(0, GY - 1)], recv.at[0, c])
-        if c + AHEAD < CH:
-            first_y(c + AHEAD)
         values = [(ybuf[c, j, 0], ybuf[c, j, 1]) for j in range(GY)]
         xsrc[c] = forward_y(values, turn_y(0), turn_y(1), table_y).reshape(GX, 8, 128)
-        over_x(1, c, lambda peer: xsrc.at[c, peer], xbuf.at[c, gx], True)
+        over_x(1, c, lambda peer: xsrc.at[c, peer], xbuf.at[c, gx], True, 0, GX - 1)
         xbuf[c, gx] = xsrc[c, gx]
 
     @pl.when(busy)
@@ -286,10 +282,12 @@
             parts = forward_x(xbuf[c].reshape(256, 128), *turn_x(c), table_i)
             for part in range(2):
                 high, low = split(parts[part])
-                ehigh[256 * part + 64 * c : 256 * part + 64 * c + 64, :] = high
-                elow[256 * part + 64 * c : 256 * part + 64 * c + 64, :] = low
-
-        spec = product((large[0], large[1]), (ehigh[...], elow[...]), NN)
+                ehigh[128 * c + 64 * part : 128 * c + 64 * part + 64, :] = high
+                elow[128 * c + 64 * part : 128 * c + 64 * part + 64, :] = low
+            if c == CH - 2:
+                head = product((large[0, :, :384], large[1, :, :384]), (ehigh[:384], elow[:384]), NN)
+
+        spec = head + product((large[0, :, 384:], large[1, :, 384:]), (ehigh[384:], elow[384:]), NN)
         scale = 0.5 / (NX * NY)
         coef_real, coef_imag = coef[0] * scale, coef[1] * scale
         real, imag = spec[:256], spec[256:]
@@ -304,8 +302,8 @@
             back = (large[2, 128 * c : 128 * c + 128, :], large[3, 128 * c : 128 * c + 128, :])
             value = product(back, (high, low), NN)
             vsrc[c] = inverse_x(value, *turn_x(c), table_i).reshape(GX, 8, 128)
+            vbuf[c, gx] = vsrc[c, gx]
             over_x(2, c, lambda peer: vsrc.at[c, peer], vbuf.at[c, gx], False)
-            vbuf[c, gx] = vsrc[c, gx]
 
     for c in range(CH):
         pl.when(busy)(lambda: wait(vbuf.at[c, pl.ds(0, BUSY - 1)], recv.at[2, c]))

time: 62.5 us -> 61.8 us (0.989)
    pallas_call x1, Pallas kernels: 60.4 us -> 59.8 us  [shards(): pl.pallas_call(kernel, out_shape=pltpu.VMEM((2, GY, 32, 128), jnp.float32...]
where the time goes in v3:
time: 61.8 us; the launch traced here: 61.6 us
  Pallas kernels  59.8 us (97%)
  other arithmetic  1.18 us (2%)
  between operations  0.68 us (1%)
    pallas_call x1, Pallas kernels, shards(): pl.pallas_call(kernel, out_shape=pltpu.VMEM((2, GY, 32, 128), jnp.float32...  59.8 us

profile of v3, /device:TPU:1, one launch (start us, length us, event | category | flops | bytes accessed | tf_op | source)
XLA Modules:
  0.0 61.6 jit_solution(15891131290016683838)
XLA Ops:
  0.7 0.0 copy-start
  0.7 59.8 %shard_map.73 = f32[2,16,32,128]{3,2,1,0:T(8,128)S(1)} custom-call(f32[2,2,16,32,128]{4,3,2,1,0:T(8,128)} %fields.1, f32[1]{0:T(128)S(6)} %copy.8.radius, f32[2]{0:T(128)} %bitcast.12, s32[1,64,1024]{2,1,0:T(8,128)} %muted.1, bf16[4,256,256]{2,1,0:T(8,128)(2,1)} %constant.8.clone.small_in, bf16[4,512,512]{2,1,0:T(8,128)(2,1)} %constant.9.clone.large_in, ...), custom_call_target="tpu_custom_call" | custom-call | tf_op jit(solution)/shard_map/pallas_call | solution.py:332
  60.4 0.0 copy-done
  60.4 0.1 fusion
  60.6 1.0 %pad_maximum_fusion = f32[2,2,16,32,128]{4,3,2,1,0:T(8,128)} fusion(f32[1,2,16,32,128]{4,3,2,1,0:T(8,128)S(1)} %get-tuple-element.6, f32[1,2,16,32,128]{4,3,2,1,0:T(8,128)S(1)} %get-tuple-element.5), kind=kLoop, calls=%fused_computation | loop fusion | flops 262144 | bytes 2097152 | tf_op jit(solution)/shard_map/stack | solution.py:361
Async XLA Ops:
  0.7 59.8 %copy-start = (f32[2,2,16,32,128]{4,3,2,1,0:T(8,128)S(1)}, f32[2,2,16,32,128]{4,3,2,1,0:T(8,128)}, u32[]{:S(2)}) copy-start(f32[2,2,16,32,128]{4,3,2,1,0:T(8,128)} %fields.1) | copy-start | bytes 3145732

commit v4 on v3

--- a/solution.py
+++ b/solution.py
@@ -155,13 +155,10 @@
         z = lax.rem(gx // 4 + 8 + jnp.where(lax.rem(turn, 2) == 1, far, -far), 8)
         return 4 * z + lax.rem(gx + 3 - lax.rem(k, 4), 4)
 
-    def early_x(k):
-        return 4 * (k // 4) + lax.rem(gx + k, 4)
-
     def early_y(k):
         step = k // 2
-        y = lax.rem(9 + jnp.where(lax.rem(step, 2) == 1, -((step + 1) // 2), step // 2), 8)
-        return 8 * lax.rem(gy // 8 + k, 2) + y
+        y = lax.rem(8 + jnp.where(lax.rem(step, 2) == 1, (step + 1) // 2, -(step // 2)), 8)
+        return 8 * lax.rem(k, 2) + y
 
     def greet_y(k, carry):
         pl.semaphore_signal(barrier, inc=1, device_id=(gx, peer_y(k)), device_id_type=MESH)
@@ -199,7 +196,7 @@
 
     def over_x(phase, c, source, target, busy_only, start=0, stop=GX):
         def one(k, carry):
-            peer = peer_x(k) if busy_only else early_x(k)
+            peer = peer_x(k) if busy_only else k
 
             def go():
                 pltpu.make_async_remote_copy(

time: 61.8 us -> 61 us (0.987)
  Pallas kernels: 59.8 us -> 58.5 us
    pallas_call x1, Pallas kernels: 59.8 us -> 58.5 us  [shards(): pl.pallas_call(kernel, out_shape=pltpu.VMEM((2, GY, 32, 128), jnp.float32...]
where the time goes in v4:
time: 61 us; the launch traced here: 60.3 us
  Pallas kernels  58.5 us (96%)
  other arithmetic  1.18 us (2%)
  between operations  0.68 us (1%)
    pallas_call x1, Pallas kernels, shards(): pl.pallas_call(kernel, out_shape=pltpu.VMEM((2, GY, 32, 128), jnp.float32...  58.5 us

profile of v4, /device:TPU:1, one launch (start us, length us, event | category | flops | bytes accessed | tf_op | source)
XLA Modules:
  0.0 60.3 jit_solution(10730397910753479433)
XLA Ops:
  0.7 0.0 copy-start
  0.7 58.5 %shard_map.73 = f32[2,16,32,128]{3,2,1,0:T(8,128)S(1)} custom-call(f32[2,2,16,32,128]{4,3,2,1,0:T(8,128)} %fields.1, f32[1]{0:T(128)S(6)} %copy.8.radius, f32[2]{0:T(128)} %bitcast.12, s32[1,64,1024]{2,1,0:T(8,128)} %muted.1, bf16[4,256,256]{2,1,0:T(8,128)(2,1)} %constant.8.clone.small_in, bf16[4,512,512]{2,1,0:T(8,128)(2,1)} %constant.9.clone.large_in, ...), custom_call_target="tpu_custom_call" | custom-call | tf_op jit(solution)/shard_map/pallas_call | solution.py:329
  59.1 0.0 copy-done
  59.1 0.1 fusion
  59.3 1.0 %pad_maximum_fusion = f32[2,2,16,32,128]{4,3,2,1,0:T(8,128)} fusion(f32[1,2,16,32,128]{4,3,2,1,0:T(8,128)S(1)} %get-tuple-element.6, f32[1,2,16,32,128]{4,3,2,1,0:T(8,128)S(1)} %get-tuple-element.5), kind=kLoop, calls=%fused_computation | loop fusion | flops 262144 | bytes 2097152 | tf_op jit(solution)/shard_map/stack | solution.py:358
Async XLA Ops:
  0.7 58.5 %copy-start = (f32[2,2,16,32,128]{4,3,2,1,0:T(8,128)S(1)}, f32[2,2,16,32,128]{4,3,2,1,0:T(8,128)}, u32[]{:S(2)}) copy-start(f32[2,2,16,32,128]{4,3,2,1,0:T(8,128)} %fields.1) | copy-start | bytes 3145732
